TPU v7x, 32 devices: a whole 2x2x4 slice. The times are simulated.
32 devices in a mesh: prow: 4 (over y, core), pcol: 8 (over z, x).
Axes of the slice: x: 2, y: 2, z: 4, core: 2. Of those that a mesh axis runs over, the one named last changes fastest.
Arguments:
- factor_rows: float32 [4096, 8192], P('prow', 'pcol'), may hold values from -128 to 128
- measurements: float32 [2048, 8192], P('prow', 'pcol'), may hold values from -256 to 256
- link_blocks: int32 [8, 12], P('prow'), may hold values from 0 to 31, all different within a row
- panel_index: int32 [1], replicated, may hold values from 0 to 30
Outputs:
- reduced_factor: float32 [4096, 8192], P('prow', 'pcol')
- reduced_measurements: float32 [2048, 8192], P('prow', 'pcol')
- panel_row: float32 [256, 8192], P(None, 'pcol')
All inputs are finite; a program needn't handle non-finite values.
Results may differ from a plain program's by a relative error of at most 0.0003.
Values sent between devices are 32-bit elements; how exact they have to be, the bound alone decides.
A program may use at most 64 MiB of HBM per device.

v0:
```python
import jax
import jax.numpy as jnp
from jax import lax
from jax.sharding import PartitionSpec as P

PB = 256
CB_DEV = 4


highest = lax.Precision.HIGHEST


def spread(block, axis, holder):
    block = jnp.where(lax.axis_index(axis) == holder, block, jnp.zeros_like(block))
    return lax.psum(block, axis)


def factor_pair(gram_matrix):
    order = gram_matrix.shape[0]
    lower_factor = jnp.linalg.cholesky(gram_matrix)
    identity = jnp.eye(order, dtype=gram_matrix.dtype)
    inverse_lower = jax.scipy.linalg.solve_triangular(lower_factor, identity, lower=True)
    return (lower_factor, inverse_lower)


def local_stack(factor_rows, measurements, link_blocks, blocks):
    touched = jnp.any(link_blocks[:, :, None] == blocks[None, None, :], axis=1)
    shaped = measurements.reshape(touched.shape[0], PB, CB_DEV, PB)
    masked = jnp.where(touched[:, None, :, None], shaped, 0.0).reshape(measurements.shape)
    return jnp.concatenate([factor_rows, masked], axis=0)


def panel_gram(panel_cols):
    return lax.psum(jnp.dot(panel_cols.T, panel_cols, precision=highest), "prow")


def summed_rows(products, finish):
    return finish(lax.psum(products, "prow"))


def local(factor_rows, measurements, link_blocks, panel_index):
    column = lax.axis_index("pcol")
    pcol_count = lax.axis_size("pcol")
    blocks = jnp.arange(CB_DEV, dtype=jnp.int32) * pcol_count + column
    stacked = local_stack(factor_rows, measurements, link_blocks, blocks)
    target = panel_index[0]
    local_slot = target // pcol_count
    owner_col = target % pcol_count
    own_panel = lax.dynamic_slice_in_dim(stacked, local_slot * PB, PB, 1)
    later_mask = jnp.repeat(blocks > target, PB)[None, :]
    panel_mask = jnp.repeat(blocks == target, PB)[None, :]
    panel_cols = spread(own_panel, "pcol", owner_col)
    lower_factor, inverse_lower = factor_pair(panel_gram(panel_cols))
    upper_factor = lower_factor.T

    def solve_left(summed):
        return jnp.dot(inverse_lower, summed, precision=highest)

    row_share = summed_rows(jnp.dot(panel_cols.T, stacked, precision=highest), solve_left)
    row_share = jnp.where(later_mask, row_share, 0.0)
    coefficients = jnp.dot(inverse_lower.T, row_share, precision=highest)
    reduced = stacked - jnp.dot(panel_cols, coefficients, precision=highest)
    panel_row = row_share + jnp.where(panel_mask, jnp.tile(upper_factor, (1, CB_DEV)), 0.0)
    split_row = factor_rows.shape[0]
    return (reduced[:split_row], reduced[split_row:], panel_row)


def solution(mesh):
    in_specs = (P("prow", "pcol"), P("prow", "pcol"), P("prow", None), P())
    out_specs = (P("prow", "pcol"), P("prow", "pcol"), P(None, "pcol"))
    return jax.shard_map(local, mesh=mesh, in_specs=in_specs, out_specs=out_specs, check_vma=False)
```

profile of v0, /device:TPU:28, one launch (start us, length us, event | category | flops | bytes accessed | tf_op | source)
XLA Modules:
  0.0 238.5 jit_solution(12730215425880428383)
XLA Ops:
  7.2 0.0 all-reduce.5.cloned.1.call-start
  7.9 0.9 compare_reduce_fusion
  8.8 0.3 broadcast_in_dim.50
  9.1 0.3 copy.14
  9.4 0.0 copy-start
  9.4 2.2 broadcast_select_fusion
  11.6 0.6 copy-done
  12.2 1.4 fusion.3
  13.6 0.0 all-reduce.5.cloned.1.call-update
  13.6 0.0 all-reduce.7.cloned.1.call-start
  13.6 88.4 %all-reduce.5.cloned.1.call-done = f32[1536,256]{1,0:T(8,128)} async-done(((f32[1536,256]{1,0:T(8,128)}), f32[1536,256]{1,0:T(8,128)}) %all-reduce.5.cloned.1.call-update) | async-done | bytes 1572880 | tf_op jit(solution)/shard_map/psum | solution.py:15
  102.0 0.0 copy-start.2
  102.0 5.3 %fusion.19 = f32[256,256]{0,1:T(8,128)} fusion(f32[1536,256]{1,0:T(8,128)} %all-reduce.5.cloned.1.call-done), kind=kOutput, calls=%fused_computation.50 | convolution fusion | flops 1207959552 | bytes 1835008 | tf_op jit(solution)/shard_map/dot_general | solution.py:34
  107.4 0.0 copy-done.2
  107.4 8.0 %fusion = f32[256,1024]{1,0:T(8,128)} fusion(f32[1536,256]{1,0:T(8,128)S(1)} %copy-done.2, f32[512,1024]{1,0:T(8,128)S(1)} %broadcast_select_fusion, f32[1024,1024]{1,0:T(8,128)} %param.4), kind=kOutput, calls=%fused_computation.5 | convolution fusion | flops 4833411072 | bytes 8912896 | tf_op jit(solution)/shard_map/dot_general | solution.py:59
  115.4 0.0 all-reduce.7.cloned.1.call-update
  115.4 0.1 broadcast_in_dim.58
  115.5 0.1 broadcast_in_dim.54
  115.6 39.1 %all-reduce.7.cloned.1.call-done = (f32[256,1024]{1,0:T(8,128)}, f32[256,256]{0,1:T(8,128)}) async-done(((f32[256,1024]{1,0:T(8,128)}, f32[256,256]{0,1:T(8,128)}), (f32[256,1024]{1,0:T(8,128)}, f32[256,256]{0,1:T(8,128)})) %all-reduce.7.cloned.1.call-update) | async-done | bytes 1310736 | tf_op jit(solution)/shard_map/psum | solution.py:38
  154.7 1.1 copy.11
  155.8 1.0 fusion.4
  156.8 11.7 %cholesky.50 = f32[128,128]{1,0:T(8,128)S(1)} custom-call(f32[128,128]{1,0:T(8,128)S(1)} %cholesky.118), custom_call_target="Cholesky" | custom-call | tf_op jit(solution)/shard_map/jit(cholesky)/cholesky | solution.py:20
  168.6 9.8 %custom-call.15 = f32[1,128,128]{1,2,0:T(8,128)S(1)} custom-call(f32[1,128,128]{2,1,0:T(8,128)S(1)} %get-tuple-element.28), custom_call_target="InvertDiagBlocksLowerTriangular" | custom-call | tf_op jit(solution)/shard_map/jit(cholesky)/cholesky | solution.py:20
  178.4 0.2 constant_dynamic-update-slice_fusion
  178.6 0.3 convolution_subtract_fusion.1
  178.9 11.7 %cholesky.105 = f32[128,128]{1,0:T(8,128)S(1)} custom-call(f32[128,128]{1,0:T(8,128)S(1)} %convolution_subtract_fusion.1), custom_call_target="Cholesky" | custom-call | tf_op jit(solution)/shard_map/jit(cholesky)/cholesky | solution.py:20
  190.6 0.6 compare_reduce_fusion.1
  192.6 0.1 copy.12
  192.8 0.1 triangular_solve.63
  192.8 4.0 %while.1 = (s32[]{:T(128)}, f32[256,256]{1,0:T(8,128)S(1)}, s32[2,2]{1,0:T(2,128)S(1)}, f32[2,128,128]{2,1,0:T(8,128)S(1)}, s32[]{:T(128)}) while((s32[]{:T(128)}, f32[256,256]{1,0:T(8,128)S(1)}, s32[2,2]{1,0:T(2,128)S(1)}, f32[2,128,128]{2,1,0:T(8,128)S(1)}, s32[]{:T(128)}) %tuple.30), condition=%wide.while_cond, body=%wide.while_body.sunk | while | flops 2 | bytes 131189 | solution.py:22
  192.8 0.6 fusion.32
  193.4 1.4 bitcast_dynamic-update-slice_fusion.2
  194.8 0.6 fusion.32
  195.4 1.4 bitcast_dynamic-update-slice_fusion.2
  196.8 19.9 %custom-call.16 = f32[2,128,128]{1,2,0:T(8,128)S(1)} custom-call(f32[2,128,128]{2,1,0:T(8,128)S(1)} %get-tuple-element.10), custom_call_target="InvertDiagBlocksLowerTriangular" | custom-call | tf_op jit(solution)/shard_map/jit(_solve_triangular)/triangular_solve | solution.py:22
  216.7 0.3 fusion.8
  217.0 0.0 copy-start.4
  217.0 0.3 convolution_subtract_fusion
  217.3 0.3 fusion.11
  217.6 0.2 tile.4
  217.8 0.2 copy.15
  218.0 0.2 copy-done.4
  218.2 0.0 copy-start.1
  218.2 2.1 select_add_fusion
  220.3 0.0 copy-start.3
  220.3 1.0 fusion.7
  221.4 0.0 copy-done.1
  221.4 0.5 copy-done.3
  221.8 5.7 %fusion.1 = f32[1536,1024]{1,0:T(8,128)S(1)} fusion(f32[512,1024]{1,0:T(8,128)S(1)} %broadcast_select_fusion, f32[1024,1024]{1,0:T(8,128)S(1)} %copy-done.1, f32[1536,256]{1,0:T(8,128)S(1)} %copy-done.3, f32[256,1024]{1,0:T(8,128)S(1)} %fusion.7), kind=kOutput, calls=%fused_computation.6 | convolution fusion | flops 4834983936 | bytes 15204352 | tf_op jit(solution)/shard_map/dot_general | solution.py:62
  227.6 1.6 slice.68
  229.1 2.5 %slice.67 = f32[1024,1024]{1,0:T(8,128)} slice(f32[1536,1024]{1,0:T(8,128)S(1)} %fusion.1), slice={[0:1024], [0:1024]} | slice | bytes 8388608 | tf_op jit(solution)/shard_map/slice | solution.py:65
  (14 shorter events, 0.2 us)
Async XLA Ops:
  7.2 94.9 %all-reduce.5.cloned.1.call-start = ((), (), s32[]{:S(2)}) async-start(), calls=%async_computation | async-start | bytes 3145728 | tf_op jit(solution)/shard_map/psum | solution.py:15
  9.4 2.8 %copy-start = (f32[1024,1024]{1,0:T(8,128)S(1)}, f32[1024,1024]{1,0:T(8,128)}, u32[]{:S(2)}) copy-start(f32[1024,1024]{1,0:T(8,128)} %param.4) | copy-start | bytes 12582916
  13.6 141.1 %all-reduce.7.cloned.1.call-start = ((), (), s32[]{:S(2)}) async-start(), calls=%async_computation.1 | async-start | bytes 2621440 | tf_op jit(solution)/shard_map/psum | solution.py:38
  102.0 5.4 %copy-start.2 = (f32[1536,256]{1,0:T(8,128)S(1)}, f32[1536,256]{1,0:T(8,128)}, u32[]{:S(2)}) copy-start(f32[1536,256]{1,0:T(8,128)} %all-reduce.5.cloned.1.call-done) | copy-start | bytes 4718596
  217.0 1.2 copy-start.4
  218.2 3.1 %copy-start.1 = (f32[1024,1024]{1,0:T(8,128)S(1)}, f32[1024,1024]{1,0:T(8,128)}, u32[]{:S(2)}) copy-start(f32[1024,1024]{1,0:T(8,128)} %param.4) | copy-start | bytes 12582916
  220.3 1.5 copy-start.3
Sparse Core Ops, SparseCore 0:
  13.7 88.2 all-reduce.4
  115.5 39.1 all-reduce.6
where the time goes:
time: 241 us; the launch traced here: 239 us
  waiting for transfers between devices  127 us (53%)
  other arithmetic  59.4 us (25%)
  matrix products  23.5 us (10%)
  between operations  16.2 us (7%)
  local copies, waits for them, and re-layouts  11.8 us (5%)
    psum x1, waiting for transfers between devices, spread(): return lax.psum(block, axis)  88.4 us
    psum x1, waiting for transfers between devices, summed_rows(): return finish(lax.psum(products, 'prow'))  39.1 us
    another operation x6, other arithmetic, factor_pair(): lower_factor = jnp.linalg.cholesky(gram_matrix)  34 us
    another operation x2, other arithmetic, factor_pair(): jax.scipy.linalg.solve_triangular(lower_factor, identity, lower=True)  19.9 us
    dot_general x1, matrix products, local(): jnp.dot(panel_cols.T, stacked, precision=highest)  8 us
    dot_general x1, matrix products, local(): reduced = stacked - jnp.dot(panel_cols, coefficients, precision=highest)  5.72 us
    dot_general x1, matrix products, panel_gram(): jnp.dot(panel_cols.T, panel_cols, precision=highest)  5.35 us
  transfers between devices with their start and end apart: 2, of which 2 were waited for; matrix products, arithmetic and copies ran while one was open for 0% of the time, Pallas kernels for 0%

commit v1 on v0

v1 whole, which is shorter than its diff:
```python
import functools
import jax, jax.numpy as jnp
from jax import lax
from jax.experimental import pallas as pl
from jax.experimental.pallas import tpu as pltpu
from jax.sharding import PartitionSpec as P

PB = 256
CB_DEV = 4
GRID_ROWS = 4
CHUNKS = 16

highest = lax.Precision.HIGHEST
high = lax.Precision.HIGH


def spread_kernel(owner, count, own_ref, panel_ref, send_sem, recv_sem):
    rows, cols = GRID_ROWS, count // GRID_ROWS
    home_r, home_c = owner // cols, owner % cols
    back_r = home_r - 1 if home_r > 0 else 1
    back_c = home_c - 1 if home_c > 0 else 1
    size = own_ref.shape[0] // (2 * CHUNKS)
    me = lax.axis_index("pcol")
    r, c = me // cols, me % cols
    same_r, same_c = r == home_r, c == home_c
    off_r, off_c = r != home_r, c != home_c
    links = (
        (r < rows - 1, cols), (r > 0, -cols), (c < cols - 1, 1), (c > 0, -1),
    )
    away = (r >= home_r, r <= home_r, c >= home_c, c <= home_c)
    fill = (
        off_c & (r == back_r) & (back_r < home_r), off_c & (r == back_r) & (back_r > home_r),
        off_r & (c == back_c) & (back_c < home_c), off_r & (c == back_c) & (back_c > home_c),
    )
    sends = (
        [links[0][0] & ((same_c & away[0]) | fill[0]), links[1][0] & ((same_c & away[1]) | fill[1]),
         links[2][0] & off_r & away[2], links[3][0] & off_r & away[3]],
        [links[0][0] & off_c & away[0], links[1][0] & off_c & away[1],
         links[2][0] & ((same_r & away[2]) | fill[2]), links[3][0] & ((same_r & away[3]) | fill[3])],
    )
    far_r, far_c = jnp.abs(r - home_r), jnp.abs(c - home_c)
    depths = (
        jnp.where(same_r & off_c, far_c + 2, far_r + far_c),
        jnp.where(same_c & off_r, far_r + 2, far_r + far_c),
    )
    mine = same_r & same_c

    @pl.when(mine)
    def _():
        panel_ref[...] = own_ref[...]

    barrier = pltpu.get_barrier_semaphore()
    for there, step in links:
        @pl.when(there)
        def _():
            pl.semaphore_signal(
                barrier, inc=1, device_id={"pcol": me + step}, device_id_type=pl.DeviceIdType.MESH
            )
    pl.semaphore_wait(barrier, sum(there.astype(jnp.int32) for there, _ in links))

    def copy(half, way, chunk):
        start = pl.multiple_of((half * CHUNKS + chunk) * size, size)
        block = panel_ref.at[pl.ds(start, size)]
        return pltpu.make_async_remote_copy(
            src_ref=block,
            dst_ref=block,
            send_sem=send_sem.at[half, way, chunk],
            recv_sem=recv_sem.at[half, chunk],
            device_id={"pcol": me + links[way][1]},
            device_id_type=pl.DeviceIdType.MESH,
        )

    def step(t, carry):
        for half in range(2):
            chunk = t - depths[half]

            @pl.when((chunk >= 0) & (chunk < CHUNKS))
            def _():
                @pl.when(jnp.logical_not(mine))
                def _():
                    copy(half, 0, chunk).wait_recv()

                for way in range(4):
                    @pl.when(sends[half][way])
                    def _():
                        copy(half, way, chunk).start()
        return carry

    lax.fori_loop(0, CHUNKS + rows + cols, step, 0)

    def finish(chunk, carry):
        for half in range(2):
            for way in range(4):
                @pl.when(sends[half][way])
                def _():
                    copy(half, way, chunk).wait_send()
        return carry

    lax.fori_loop(0, CHUNKS, finish, 0)


def spread(own, owner, count):
    def from_owner(index):
        return pl.pallas_call(
            functools.partial(spread_kernel, index, count),
            out_shape=jax.ShapeDtypeStruct(own.shape, own.dtype),
            in_specs=[pl.BlockSpec(memory_space=pltpu.VMEM)],
            out_specs=pl.BlockSpec(memory_space=pltpu.VMEM),
            scratch_shapes=[
                pltpu.SemaphoreType.DMA((2, 4, CHUNKS)),
                pltpu.SemaphoreType.DMA((2, CHUNKS)),
            ],
            compiler_params=pltpu.CompilerParams(
                collective_id=index, has_side_effects=True, vmem_limit_bytes=16 << 20
            ),
        )

    return lax.switch(owner, [from_owner(index) for index in range(count)], own)


def eliminate(square, width, group):
    identity = (
        lax.broadcasted_iota(jnp.int32, (width, width), 0)
        == lax.broadcasted_iota(jnp.int32, (width, width), 1)
    ).astype(jnp.float32)
    strips = [jnp.concatenate([square[k:k + 8], identity[k:k + 8]], axis=1) for k in range(0, width, 8)]
    lanes = 2 * width
    for start in range(0, width, group):
        first = start // 8
        columns = []
        for j in range(start, start + group):
            columns.append([jnp.broadcast_to(strips[s][:, j:j + 1], (8, lanes)) for s in range(first, len(strips))])
        for k in range(group):
            j = start + k
            own, row = j // 8 - first, j % 8
            inverse = 1.0 / columns[k][own][row:row + 1]
            pivot_row = strips[j // 8][row:row + 1] * inverse
            below = lax.broadcasted_iota(jnp.int32, (8, lanes), 0) > row
            factors = [columns[k][s] if s > own else jnp.where(below, columns[k][s], 0.0) for s in range(own, len(columns[k]))]
            for l in range(k + 1, group):
                scale = columns[l][own][row:row + 1] * inverse
                for s in range(own, len(columns[l])):
                    columns[l][s] = columns[l][s] - factors[s - own] * scale
            for s in range(own, len(columns[k])):
                strips[first + s] = strips[first + s] - factors[s - own] * pivot_row
    whole = jnp.concatenate(strips, axis=0)
    pivots = jnp.sum(whole[:, :width] * identity, axis=1, keepdims=True)
    whole = whole * (1.0 / jnp.sqrt(pivots))
    return whole[:, width:]

def factor_kernel(width, group, gram_ref, upper_ref, inverse_ref, work):
    order = gram_ref.shape[0]
    work[...] = gram_ref[...]
    column = lax.broadcasted_iota(jnp.int32, (width, order), 1)
    for start in range(0, order, width):
        stop = start + width
        block_inverse = eliminate(work[start:stop, start:stop], width, group)
        rows = jnp.dot(block_inverse, work[start:stop, :], precision=highest, preferred_element_type=jnp.float32)
        upper = jnp.where(column >= start + lax.broadcasted_iota(jnp.int32, (width, order), 0), rows, 0.0)
        upper_ref[start:stop, :] = upper
        pad = [jnp.zeros((width, start), jnp.float32)] * (start > 0) + [block_inverse]
        pad += [jnp.zeros((width, order - stop), jnp.float32)] * (stop < order)
        placed = jnp.concatenate(pad, axis=1) if len(pad) > 1 else pad[0]
        inverse = jnp.where(column < start, rows, placed)
        inverse_ref[start:stop, :] = inverse
        if stop < order:
            inside = (column >= start) & (column < stop)
            rows = jnp.where(inside, placed, rows)
            rest = work[stop:, :]
            rest_column = lax.broadcasted_iota(jnp.int32, rest.shape, 1)
            rest = jnp.where((rest_column >= start) & (rest_column < stop), 0.0, rest)
            taken = lax.dot_general(upper, rows, (((0,), (0,)), ((), ())), precision=highest, preferred_element_type=jnp.float32)
            work[stop:, :] = rest - taken[stop:, :]

def factor(gram, width=64, group=8):
    order = gram.shape[0]
    shape = jax.ShapeDtypeStruct((order, order), jnp.float32)
    return pl.pallas_call(
        functools.partial(factor_kernel, width, group),
        out_shape=(shape, shape),
        in_specs=[pl.BlockSpec(memory_space=pltpu.VMEM)],
        out_specs=[pl.BlockSpec(memory_space=pltpu.VMEM)] * 2,
        scratch_shapes=[pltpu.VMEM((order, order), jnp.float32)],
        compiler_params=pltpu.CompilerParams(vmem_limit_bytes=32 << 20),
        cost_estimate=pl.CostEstimate(flops=2000000000, bytes_accessed=800000, transcendentals=0),
    )(gram)


def exchange_sum(partial, axis):
    count = lax.axis_size(axis)
    distance = 1
    while distance < count:
        pairs = [(i, i ^ distance) for i in range(count)]
        partial = partial + lax.ppermute(partial, axis, pairs)
        distance *= 2
    return partial


def products(left, right, precision):
    return lax.dot_general(left, right, (((0,), (0,)), ((), ())), precision=precision)


def local(factor_rows, measurements, link_blocks, panel_index):
    column = lax.axis_index("pcol")
    count = lax.axis_size("pcol")
    blocks = jnp.arange(CB_DEV, dtype=jnp.int32) * count + column
    touched = jnp.any(link_blocks[:, :, None] == blocks[None, None, :], axis=1)
    shaped = measurements.reshape(touched.shape[0], PB, CB_DEV, PB)
    masked = jnp.where(touched[:, None, :, None], shaped, 0.0).reshape(measurements.shape)
    split_row = factor_rows.shape[0]
    target = panel_index[0]
    slot, owner = target // count, target % count
    own = jnp.concatenate([
        lax.dynamic_slice_in_dim(factor_rows, slot * PB, PB, 1),
        lax.dynamic_slice_in_dim(masked, slot * PB, PB, 1),
    ], axis=0)
    later = jnp.repeat(blocks > target, PB)[None, :]
    at_panel = jnp.repeat(blocks == target, PB)[None, :]
    panel = spread(own, owner, count)
    panel_f, panel_m = panel[:split_row], panel[split_row:]
    gram = exchange_sum(products(panel, panel, highest), "prow")
    upper, inverse_lower = factor(gram)
    cross = products(panel_f, factor_rows, high) + products(panel_m, masked, high)
    cross = exchange_sum(cross, "prow")
    share = jnp.where(later, jnp.dot(inverse_lower, cross, precision=highest), 0.0)
    coefficients = products(inverse_lower, share, highest)
    reduced_f = factor_rows - jnp.dot(panel_f, coefficients, precision=high)
    reduced_m = masked - jnp.dot(panel_m, coefficients, precision=high)
    panel_row = share + jnp.where(at_panel, jnp.tile(upper, (1, CB_DEV)), 0.0)
    return (reduced_f, reduced_m, panel_row)


def solution(mesh):
    in_specs = (P("prow", "pcol"), P("prow", "pcol"), P("prow", None), P())
    out_specs = (P("prow", "pcol"), P("prow", "pcol"), P(None, "pcol"))
    return jax.shard_map(local, mesh=mesh, in_specs=in_specs, out_specs=out_specs, check_vma=False)
```

time: 241 us -> 124 us (0.51)
  waiting for transfers between devices: 127 us -> 28.4 us
  Pallas kernels: 0 us -> 64.4 us
  other arithmetic: 59.4 us -> 1.54 us
  between operations: 16.2 us -> 1.49 us
  local copies, waits for them, and re-layouts: 11.8 us -> 4.77 us
  matrix products: 23.5 us -> 20.5 us
    psum x2 -> x0, waiting for transfers between devices: 127 us -> none  [the longest x1 88.4 us: spread(): return lax.psum(block, axis)]
    pallas_call x0 -> x2, Pallas kernels: none -> 64.4 us  [the longest x1 55.3 us: spread(): return lax.switch(owner, [from_owner(index) for index in range(count)], own)]
    another operation x8 -> x0, other arithmetic: 53.9 us -> none  [the longest x6 34 us: factor_pair(): lower_factor = jnp.linalg.cholesky(gram_matrix)]
    ppermute x0 -> x4, waiting for transfers between devices: none -> 28.4 us  [exchange_sum(): partial = partial + lax.ppermute(partial, axis, pairs)]
    slice x2 -> x0, local copies, waits for them, and re-layouts: 4.11 us -> none  [local(): return (reduced[:split_row], reduced[split_row:], panel_row)]
    another operation x10 -> x1, local copies, waits for them, and re-layouts: 4.23 us -> 0.18 us  [local(): panel_row = share + jnp.where(at_panel, jnp.tile(upper, (1, CB_DEV)), 0.0)]
    select_n x2 -> x1, other arithmetic: 3.59 us -> 0.34 us  [local(): jnp.where(touched[:, None, :, None], shaped, 0.0)]
    dot_general x5 -> x7, matrix products: 22.2 us -> 20.5 us  [the longest x4 10.5 us: products(): lax.dot_general(left, right, (((0,), (0,)), ((), ())), precision=precision)]
  transfers between devices with their start and end apart: 2 -> 4, of which waited for: 2 -> 3; matrix products, arithmetic and copies ran while one was open for 0% -> 3% of each run, Pallas kernels for 0% -> 7%
where the time goes in v1:
time: 124 us
  Pallas kernels  64.4 us (52%)
  waiting for transfers between devices  28.4 us (23%)
  matrix products  20.5 us (17%)
  local copies, waits for them, and re-layouts  4.77 us (4%)
  starting transfers between devices  2.3 us (2%)
  other arithmetic  1.54 us (1%)
  between operations  1.49 us (1%)
    pallas_call x1, Pallas kernels, spread(): return lax.switch(owner, [from_owner(index) for index in range(count)], own)  55.3 us
    ppermute x4, waiting for transfers between devices, exchange_sum(): partial = partial + lax.ppermute(partial, axis, pairs)  28.4 us
    dot_general x4, matrix products, products(): lax.dot_general(left, right, (((0,), (0,)), ((), ())), precision=precision)  10.5 us
    pallas_call x1, Pallas kernels, factor(): pl.pallas_call(functools.partial(factor_kernel, width, group), out_shape=...  9.18 us
    dot_general x1, matrix products, local(): reduced_f = factor_rows - jnp.dot(panel_f, coefficients, precision=high)  4.03 us
    dot_general x1, matrix products, local(): jnp.dot(inverse_lower, cross, precision=highest)  3.56 us
    unnamed x10, local copies, waits for them, and re-layouts  2.59 us
  transfers between devices with their start and end apart: 4, of which 3 were waited for; matrix products, arithmetic and copies ran while one was open for 3% of the time, Pallas kernels for 7%

profile of v1, /device:TPU:28, one launch (start us, length us, event | category | flops | bytes accessed | tf_op | source)
XLA Modules:
  0.0 123.7 jit_solution(1169406310013681600)
XLA Ops:
  1.3 0.9 compare_reduce_fusion
  2.2 0.3 broadcast_in_dim.45
  2.5 0.0 copy-start.3
  2.5 0.3 copy.7
  2.8 1.4 %constant_dynamic-slice_fusion.1 = f32[1024,256]{1,0:T(8,128)S(1)} fusion(f32[1024,1024]{1,0:T(8,128)} %param.12, s32[]{:T(128)S(6)} %select_n.29), kind=kLoop, calls=%fused_computation.16 | loop fusion | bytes 2097156 | tf_op jit(solution)/shard_map/dynamic_slice | solution.py:214
  4.3 0.2 copy-done.3
  4.5 0.3 broadcast_select_fusion
  4.8 0.0 copy-start
  4.8 1.3 %copy-done = f32[512,1024]{1,0:T(8,128)} copy-done((f32[512,1024]{1,0:T(8,128)}, f32[512,1024]{1,0:T(8,128)S(1)}, u32[]{:S(2)}) %copy-start) | copy-done | bytes 2097176
  6.2 0.1 pad_maximum_fusion
  6.3 55.5 %conditional.1 = (f32[1536,256]{1,0:T(8,128)S(1)}) conditional(s32[]{:T(128)} %clamp.3, f32[1536,256]{1,0:T(8,128)S(1)} %pad_maximum_fusion, f32[1536,256]{1,0:T(8,128)S(1)} %pad_maximum_fusion, f32[1536,256]{1,0:T(8,128)S(1)} %pad_maximum_fusion, f32[1536,256]{1,0:T(8,128)S(1)} %pad_maximum_fusion, ...), branch_computations={%region_1.2_spmd, %region_2.3_spmd, %region_3.4_spmd, %region_4.5_... | conditional | bytes 8 | solution.py:118
  6.3 55.3 %branch_0_fun.1 = f32[1536,256]{1,0:T(8,128)S(1)} custom-call(f32[1536,256]{1,0:T(8,128)S(1)} %own_ref), custom_call_target="tpu_custom_call" | custom-call | tf_op jit(solution)/shard_map/cond/branch_0_fun/pallas_call | solution.py:118
  61.8 2.7 %fusion.4 = f32[256,1024]{1,0:T(8,128)S(1)} fusion(f32[512,1024]{1,0:T(8,128)} %copy-done, f32[1536,256]{1,0:T(8,128)S(1)} %get-tuple-element.34), kind=kOutput, calls=%fused_computation.11 | convolution fusion | flops 805306368 | bytes 3670016 | tf_op jit(solution)/shard_map/dot_general | solution.py:200
  64.4 4.1 %convolution_add_fusion = f32[256,1024]{1,0:T(8,128)S(1)} fusion(f32[256,1024]{1,0:T(8,128)S(1)} %fusion.4, f32[1024,1024]{1,0:T(8,128)} %param.12, f32[1536,256]{1,0:T(8,128)S(1)} %get-tuple-element.34), kind=kOutput, calls=%fused_computation.4 | convolution fusion | flops 1610874880 | bytes 7340032 | tf_op jit(solution)/shard_map/dot_general | solution.py:200
  68.6 0.1 collective-permute-start.2
  68.6 2.6 %collective-permute-done.2 = f32[256,1024]{1,0:T(8,128)S(1)} collective-permute-done((f32[256,1024]{1,0:T(8,128)S(1)}, f32[256,1024]{1,0:T(8,128)S(1)}, u32[]{:S(2)}, u32[]{:S(2)}) %collective-permute-start.2) | collective-permute-done | bytes 1048608 | tf_op jit(solution)/shard_map/ppermute | solution.py:194
  71.3 0.2 add.44
  71.5 0.6 collective-permute-start.3
  72.0 2.7 %fusion.6 = f32[256,256]{1,0:T(8,128)S(1)} fusion(f32[1536,256]{1,0:T(8,128)S(1)} %get-tuple-element.34), kind=kOutput, calls=%fused_computation.19 | convolution fusion | flops 1207959552 | bytes 1835008 | tf_op jit(solution)/shard_map/dot_general | solution.py:200
  74.7 0.1 collective-permute-start
  74.8 1.5 %collective-permute-done = f32[256,256]{1,0:T(8,128)S(1)} collective-permute-done((f32[256,256]{1,0:T(8,128)S(1)}, f32[256,256]{1,0:T(8,128)S(1)}, u32[]{:S(2)}, u32[]{:S(2)}) %collective-permute-start) | collective-permute-done | bytes 262176 | tf_op jit(solution)/shard_map/ppermute | solution.py:194
  76.3 1.6 %collective-permute-start.1 = (f32[256,256]{1,0:T(8,128)S(1)}, f32[256,256]{1,0:T(8,128)S(1)}, u32[]{:S(2)}, u32[]{:S(2)}) collective-permute-start(f32[256,256]{1,0:T(8,128)S(1)} %add.41), channel_id=1, source_target_pairs={{0,16},{8,24},{16,0},{24,8},{1,17},{9,25},{17,1},{25,9},{2,18},{10... | collective-permute-start | bytes 786440 | tf_op jit(solution)/shard_map/ppermute | solution.py:194
  77.9 0.1 broadcast_in_dim.52
  78.0 0.1 broadcast_in_dim.48
  78.1 24.2 %collective-permute-done.1 = f32[256,256]{1,0:T(8,128)S(1)} collective-permute-done((f32[256,256]{1,0:T(8,128)S(1)}, f32[256,256]{1,0:T(8,128)S(1)}, u32[]{:S(2)}, u32[]{:S(2)}) %collective-permute-start.1) | collective-permute-done | bytes 262176 | tf_op jit(solution)/shard_map/ppermute | solution.py:194
  102.4 9.2 %shard_map.67 = (f32[256,256]{1,0:T(8,128)S(1)}, f32[256,256]{1,0:T(8,128)S(1)}) custom-call(f32[256,256]{1,0:T(8,128)S(1)} %add.42.gram_ref), custom_call_target="tpu_custom_call" | custom-call | flops 2000000000 | bytes 800000 | tf_op jit(solution)/shard_map/pallas_call | solution.py:178
  111.6 0.2 tile.4
  111.7 0.2 copy.8
  112.0 0.0 collective-permute-done.3
  112.0 3.6 %select_add_fusion = (f32[256,1024]{1,0:T(8,128)}, f32[256,1024]{1,0:T(8,128)S(1)}) fusion(f32[256,1024]{1,0:T(8,128)S(1)} %bitcast.20, pred[1024]{0:T(1024)(128)(4,1)S(1)} %broadcast_in_dim.53, f32[256,256]{1,0:T(8,128)S(1)} %get-tuple-element.28, f32[256,1024]{1,0:T(8,128)S(1)} %add.44, f32[256,1024]{1,0:T(8,128)} %collective-permute-done.3, ...), kind=kOutput, calls=%fused_computation.5 | convolution fusion | flops 806354944 | bytes 5507072 | tf_op jit(solution)/shard_map/dot_general | solution.py:225
  115.5 0.0 copy-start.1
  115.5 1.0 fusion.7
  116.6 0.5 copy-done.1
  117.1 0.0 copy-start.2
  117.1 2.4 %convolution_subtract_fusion.1 = f32[512,1024]{1,0:T(8,128)} fusion(f32[512,1024]{1,0:T(8,128)S(1)} %copy-done.1, f32[256,1024]{1,0:T(8,128)S(1)} %fusion.7, f32[1536,256]{1,0:T(8,128)S(1)} %get-tuple-element.34), kind=kOutput, calls=%fused_computation.1 | convolution fusion | flops 805830656 | bytes 5767168 | tf_op jit(solution)/shard_map/dot_general | solution.py:228
  119.5 0.1 copy-done.2
  119.6 4.0 %convolution_subtract_fusion = f32[1024,1024]{1,0:T(8,128)} fusion(f32[1024,1024]{1,0:T(8,128)S(1)} %copy-done.2, f32[256,1024]{1,0:T(8,128)S(1)} %fusion.7, f32[1536,256]{1,0:T(8,128)S(1)} %get-tuple-element.34), kind=kOutput, calls=%fused_computation | convolution fusion | flops 1611661312 | bytes 10485760 | tf_op jit(solution)/shard_map/dot_general | solution.py:227
  (7 shorter events, 0.1 us)
Async XLA Ops:
  2.5 1.9 %copy-start.3 = (f32[512,1024]{1,0:T(8,128)S(1)}, f32[512,1024]{1,0:T(8,128)}, u32[]{:S(2)}) copy-start(f32[512,1024]{1,0:T(8,128)} %param.13) | copy-start | bytes 6291460
  4.8 1.3 %copy-start = (f32[512,1024]{1,0:T(8,128)}, f32[512,1024]{1,0:T(8,128)S(1)}, u32[]{:S(2)}) copy-start(f32[512,1024]{1,0:T(8,128)S(1)} %broadcast_select_fusion) | copy-start | bytes 6291460
  68.6 2.7 %collective-permute-start.2 = (f32[256,1024]{1,0:T(8,128)S(1)}, f32[256,1024]{1,0:T(8,128)S(1)}, u32[]{:S(2)}, u32[]{:S(2)}) collective-permute-start(f32[256,1024]{1,0:T(8,128)S(1)} %convolution_add_fusion), channel_id=1, source_target_pairs={{0,8},{8,0},{16,24},{24,16},{1,9},{9,1},{17,25},{25,17},{2,10},{10... | collective-permute-start | bytes 3145736 | tf_op jit(solution)/shard_map/ppermute | solution.py:194
  71.5 40.5 %collective-permute-start.3 = (f32[256,1024]{1,0:T(8,128)S(1)}, f32[256,1024]{1,0:T(8,128)}, u32[]{:S(2)}, u32[]{:S(2)}) collective-permute-start(f32[256,1024]{1,0:T(8,128)S(1)} %add.44), channel_id=1, source_target_pairs={{0,16},{8,24},{16,0},{24,8},{1,17},{9,25},{17,1},{25,9},{2,18},{10... | collective-permute-start | bytes 3145736 | tf_op jit(solution)/shard_map/ppermute | solution.py:194
  74.7 1.6 %collective-permute-start = (f32[256,256]{1,0:T(8,128)S(1)}, f32[256,256]{1,0:T(8,128)S(1)}, u32[]{:S(2)}, u32[]{:S(2)}) collective-permute-start(f32[256,256]{1,0:T(8,128)S(1)} %fusion.6), channel_id=1, source_target_pairs={{0,8},{8,0},{16,24},{24,16},{1,9},{9,1},{17,25},{25,17},{2,10},{10... | collective-permute-start | bytes 786440 | tf_op jit(solution)/shard_map/ppermute | solution.py:194
  76.3 26.0 %collective-permute-start.1 = (f32[256,256]{1,0:T(8,128)S(1)}, f32[256,256]{1,0:T(8,128)S(1)}, u32[]{:S(2)}, u32[]{:S(2)}) collective-permute-start(f32[256,256]{1,0:T(8,128)S(1)} %add.41), channel_id=1, source_target_pairs={{0,16},{8,24},{16,0},{24,8},{1,17},{9,25},{17,1},{25,9},{2,18},{10... | collective-permute-start | bytes 786440 | tf_op jit(solution)/shard_map/ppermute | solution.py:194
  115.5 1.6 %copy-start.1 = (f32[512,1024]{1,0:T(8,128)S(1)}, f32[512,1024]{1,0:T(8,128)}, u32[]{:S(2)}) copy-start(f32[512,1024]{1,0:T(8,128)} %copy-done) | copy-start | bytes 6291460
  117.1 2.5 %copy-start.2 = (f32[1024,1024]{1,0:T(8,128)S(1)}, f32[1024,1024]{1,0:T(8,128)}, u32[]{:S(2)}) copy-start(f32[1024,1024]{1,0:T(8,128)} %param.12) | copy-start | bytes 12582916
